TPU v7x, 32 devices: a whole 2x2x4 slice. The times are simulated.
32 devices in a mesh: dp: 8 (over y, x, core), seq: 4 (over z).
Axes of the slice: x: 2, y: 2, z: 4, core: 2. Of those that a mesh axis runs over, the one named last changes fastest.
Arguments:
- queries: bfloat16 [4096, 1280], P(('dp', 'seq')), may hold values from -6 to 6
- key_states: bfloat16 [4096, 1280], P(('dp', 'seq')), may hold values from -6 to 6
- value_states: bfloat16 [4096, 1280], P(('dp', 'seq')), may hold values from -6 to 6
- out_grads: bfloat16 [4096, 1280], P(('dp', 'seq')), may hold values from -6 to 6
- row_order: int32 [4096], P(('dp', 'seq')), may hold values from 0 to 127, as said below
- segment_ids: int32 [8, 512], P('dp'), may hold values from 0 to 1, as said below
Outputs:
- grad_queries: bfloat16 [4096, 1280], P(('dp', 'seq'))
- grad_keys: bfloat16 [4096, 1280], P(('dp', 'seq'))
- grad_values: bfloat16 [4096, 1280], P(('dp', 'seq'))
Inputs may be any that keep to these rules, and one draw needn't show every extreme that they name: `row_order`: each block of 128 entries names every number of 0 to 127 once. `segment_ids`: each row holds two screenshots: ids 0 then 1, never falling; the first row with id 1 lies between 192 and 320.
All inputs are finite; a program needn't handle non-finite values.
Results may differ from a plain program's by a relative error of at most 0.012.
Values may be sent and summed in bfloat16 or wider, within the bound.
No kernel may reach another device: no remote copies, remote signals or barrier semaphores. Data moves between devices by JAX's collectives and lax.ppermute only.
A program may use at most 64 MiB of HBM per device.

v0:
```python
import math

import jax
import jax.numpy as jnp
from jax import lax
from jax.sharding import PartitionSpec as P

HD = 80


NEG_FILL = -1e30


def block_count(length):
    return max(1, length // 512)


def score_block(query_block, key_block, query_seg, key_seg, inv_root):
    scores = (
        jnp.einsum("qhd,khd->hqk", query_block, key_block, preferred_element_type=jnp.float32)
        * inv_root
    )
    matched = query_seg[:, None] == key_seg[None, :]
    return jnp.where(matched[None], scores, NEG_FILL)


def row_delta(grad_block, attended):
    return jnp.sum(grad_block.astype(jnp.float32) * attended, axis=-1).T[:, :, None]


def skip_grads(query_rows, key_rows, value_rows, grad_rows, query_seg, key_seg, inv_root):
    rows, heads, width = query_rows.shape
    key_count = key_rows.shape[0]
    blocks = block_count(rows)
    span = rows // blocks
    key_blocks = block_count(key_count)
    key_span = key_count // key_blocks

    def key_piece(array, key_index):
        return lax.dynamic_slice_in_dim(array, key_index * key_span, key_span, 0)

    def visit(block_index, carry):
        grad_q, grad_k, grad_v = carry
        start = block_index * span
        query_block = lax.dynamic_slice_in_dim(query_rows, start, span, 0)
        grad_block = lax.dynamic_slice_in_dim(grad_rows, start, span, 0)
        seg_block = lax.dynamic_slice_in_dim(query_seg, start, span, 0)

        def touches(key_index):
            seg_piece = key_piece(key_seg, key_index)
            return (seg_block[0] <= seg_piece[-1]) & (seg_piece[0] <= seg_block[-1])

        def scores_of(key_index):
            return score_block(
                query_block,
                key_piece(key_rows, key_index),
                seg_block,
                key_piece(key_seg, key_index),
                inv_root,
            )

        def stats_step(key_index, state):

            def stats_update(state):
                top, total = state
                scores = scores_of(key_index)
                new_top = jnp.maximum(top, jnp.max(scores, axis=-1, keepdims=True))
                total = total * jnp.exp(top - new_top) + jnp.sum(
                    jnp.exp(scores - new_top), axis=-1, keepdims=True
                )
                return (new_top, total)

            return lax.cond(touches(key_index), stats_update, lambda state: state, state)

        top, total = lax.fori_loop(
            0,
            key_blocks,
            stats_step,
            (
                jnp.full((heads, span, 1), NEG_FILL, jnp.float32),
                jnp.zeros((heads, span, 1), jnp.float32),
            ),
        )

        def output_step(key_index, attended):

            def output_update(attended):
                probs = jnp.exp(scores_of(key_index) - top) / total
                return attended + jnp.einsum(
                    "hqk,khd->qhd",
                    probs.astype(jnp.bfloat16),
                    key_piece(value_rows, key_index),
                    preferred_element_type=jnp.float32,
                )

            return lax.cond(touches(key_index), output_update, lambda attended: attended, attended)

        attended = lax.fori_loop(
            0, key_blocks, output_step, jnp.zeros((span, heads, width), jnp.float32)
        )
        delta = row_delta(grad_block, attended)

        def grad_step(key_index, state):

            def grad_update(state):
                acc_q, acc_k, acc_v = state
                key_block = key_piece(key_rows, key_index)
                value_block = key_piece(value_rows, key_index)
                probs = jnp.exp(scores_of(key_index) - top) / total
                probs_low = probs.astype(jnp.bfloat16)
                dprobs = jnp.einsum(
                    "qhd,khd->hqk", grad_block, value_block, preferred_element_type=jnp.float32
                )
                dscores = (probs * (dprobs - delta) * inv_root).astype(jnp.bfloat16)
                acc_q = acc_q + jnp.einsum(
                    "hqk,khd->qhd", dscores, key_block, preferred_element_type=jnp.float32
                )
                key_start = key_index * key_span
                new_k = key_piece(acc_k, key_index) + jnp.einsum(
                    "hqk,qhd->khd", dscores, query_block, preferred_element_type=jnp.float32
                )
                new_v = key_piece(acc_v, key_index) + jnp.einsum(
                    "hqk,qhd->khd", probs_low, grad_block, preferred_element_type=jnp.float32
                )
                acc_k = lax.dynamic_update_slice_in_dim(acc_k, new_k, key_start, 0)
                acc_v = lax.dynamic_update_slice_in_dim(acc_v, new_v, key_start, 0)
                return (acc_q, acc_k, acc_v)

            return lax.cond(touches(key_index), grad_update, lambda state: state, state)

        acc_q, grad_k, grad_v = lax.fori_loop(
            0, key_blocks, grad_step, (jnp.zeros((span, heads, width), jnp.float32), grad_k, grad_v)
        )
        grad_q = lax.dynamic_update_slice_in_dim(grad_q, acc_q.astype(jnp.bfloat16), start, 0)
        return (grad_q, grad_k, grad_v)

    start_state = (
        jnp.zeros(query_rows.shape, jnp.bfloat16),
        jnp.zeros(key_rows.shape, jnp.float32),
        jnp.zeros(key_rows.shape, jnp.float32),
    )
    return lax.fori_loop(0, blocks, visit, start_state)


def on_device(queries, key_states, value_states, out_grads, row_order, segment_ids):
    rows = queries.shape[0]
    heads = queries.shape[1] // HD
    inv_root = 1.0 / math.sqrt(HD)
    group_seg = segment_ids[0]
    permuted = (
        queries[row_order],
        key_states[row_order],
        value_states[row_order],
        out_grads[row_order],
    )
    moved = (
        lax.all_to_all(permuted[0], "dp", split_axis=0, concat_axis=0, tiled=True),
        lax.all_to_all(permuted[1], "dp", split_axis=0, concat_axis=0, tiled=True),
        lax.all_to_all(permuted[2], "dp", split_axis=0, concat_axis=0, tiled=True),
        lax.all_to_all(permuted[3], "dp", split_axis=0, concat_axis=0, tiled=True),
    )
    shaped = tuple((item.reshape(rows, heads, HD) for item in moved))
    seq_devs = lax.axis_size("seq")
    own_heads = heads // seq_devs
    split_form = tuple((item.reshape(rows, seq_devs, own_heads, HD) for item in shaped))
    parts = (
        lax.all_to_all(split_form[0], "seq", split_axis=1, concat_axis=0, tiled=True),
        lax.all_to_all(split_form[1], "seq", split_axis=1, concat_axis=0, tiled=True),
        lax.all_to_all(split_form[2], "seq", split_axis=1, concat_axis=0, tiled=True),
        lax.all_to_all(split_form[3], "seq", split_axis=1, concat_axis=0, tiled=True),
    )
    flat_parts = tuple((part[:, 0] for part in parts))
    grads = skip_grads(
        flat_parts[0], flat_parts[1], flat_parts[2], flat_parts[3], group_seg, group_seg, inv_root
    )
    grad_q, grad_k, grad_v = (
        lax.all_to_all(grads[0][:, None], "seq", split_axis=0, concat_axis=1, tiled=True),
        lax.all_to_all(
            grads[1].astype(jnp.bfloat16)[:, None], "seq", split_axis=0, concat_axis=1, tiled=True
        ),
        lax.all_to_all(
            grads[2].astype(jnp.bfloat16)[:, None], "seq", split_axis=0, concat_axis=1, tiled=True
        ),
    )
    flat = (
        grad_q.reshape(rows, heads * HD),
        grad_k.reshape(rows, heads * HD),
        grad_v.reshape(rows, heads * HD),
    )
    returned = (
        lax.all_to_all(flat[0], "dp", split_axis=0, concat_axis=0, tiled=True),
        lax.all_to_all(flat[1], "dp", split_axis=0, concat_axis=0, tiled=True),
        lax.all_to_all(flat[2], "dp", split_axis=0, concat_axis=0, tiled=True),
    )
    positions = jnp.arange(rows, dtype=jnp.int32)
    inverse = jnp.zeros_like(row_order).at[row_order].set(positions)
    return (returned[0][inverse], returned[1][inverse], returned[2][inverse])


def solution(mesh):
    placed = (
        P(("dp", "seq"), None),
        P(("dp", "seq"), None),
        P(("dp", "seq"), None),
        P(("dp", "seq"), None),
        P(("dp", "seq")),
        P("dp", None),
    )
    return jax.shard_map(
        on_device,
        mesh=mesh,
        in_specs=placed,
        out_specs=(P(("dp", "seq"), None), P(("dp", "seq"), None), P(("dp", "seq"), None)),
        check_vma=False,
    )
```

profile of v0, /device:TPU:1, one launch (start us, length us, event | category | flops | bytes accessed | tf_op | source)
XLA Modules:
  0.0 183.5 jit_solution(10967556386163505686)
XLA Ops:
  0.7 0.7 compare_select_fusion.1
  1.6 1.6 gather_fusion.3
  3.2 5.4 %all-to-all-start.6 = ((bf16[8,16,1280]{2,1,0:T(8,128)(2,1)}), bf16[8,16,1280]{2,1,0:T(8,128)(2,1)S(1)}, u32[]{:S(2)}, u32[]{:S(2)}) async-start(bf16[8,16,1280]{2,1,0:T(8,128)(2,1)} %bitcast.22), calls=%async_computation.6 | async-start | bytes 655360 | tf_op jit(solution)/shard_map/all_to_all | solution.py:159
  8.6 1.6 gather_fusion.2
  10.2 4.3 %all-to-all-done.6 = bf16[8,16,1280]{2,1,0:T(8,128)(2,1)S(1)} async-done(((bf16[8,16,1280]{2,1,0:T(8,128)(2,1)}), bf16[8,16,1280]{2,1,0:T(8,128)(2,1)S(1)}, u32[]{:S(2)}, u32[]{:S(2)}) %all-to-all-start.6) | async-done | bytes 327712 | tf_op jit(solution)/shard_map/all_to_all | solution.py:159
  14.5 5.0 %all-to-all-start.4 = ((bf16[8,16,1280]{2,1,0:T(8,128)(2,1)}), bf16[8,16,1280]{2,1,0:T(8,128)(2,1)S(1)}, u32[]{:S(2)}, u32[]{:S(2)}) async-start(bf16[8,16,1280]{2,1,0:T(8,128)(2,1)} %bitcast.19), calls=%async_computation.4 | async-start | bytes 655360 | tf_op jit(solution)/shard_map/all_to_all | solution.py:160
  19.6 1.6 gather_fusion.1
  21.2 4.4 %all-to-all-done.4 = bf16[8,16,1280]{2,1,0:T(8,128)(2,1)S(1)} async-done(((bf16[8,16,1280]{2,1,0:T(8,128)(2,1)}), bf16[8,16,1280]{2,1,0:T(8,128)(2,1)S(1)}, u32[]{:S(2)}, u32[]{:S(2)}) %all-to-all-start.4) | async-done | bytes 327712 | tf_op jit(solution)/shard_map/all_to_all | solution.py:160
  25.6 5.0 %all-to-all-start.2 = ((bf16[8,16,1280]{2,1,0:T(8,128)(2,1)}), bf16[8,16,1280]{2,1,0:T(8,128)(2,1)S(1)}, u32[]{:S(2)}, u32[]{:S(2)}) async-start(bf16[8,16,1280]{2,1,0:T(8,128)(2,1)} %bitcast.16), calls=%async_computation.2 | async-start | bytes 655360 | tf_op jit(solution)/shard_map/all_to_all | solution.py:158
  30.6 1.6 gather_fusion
  32.2 4.4 %all-to-all-done.2 = bf16[8,16,1280]{2,1,0:T(8,128)(2,1)S(1)} async-done(((bf16[8,16,1280]{2,1,0:T(8,128)(2,1)}), bf16[8,16,1280]{2,1,0:T(8,128)(2,1)S(1)}, u32[]{:S(2)}, u32[]{:S(2)}) %all-to-all-start.2) | async-done | bytes 327712 | tf_op jit(solution)/shard_map/all_to_all | solution.py:158
  36.6 5.0 %all-to-all-start = ((bf16[8,16,1280]{2,1,0:T(8,128)(2,1)}), bf16[8,16,1280]{2,1,0:T(8,128)(2,1)S(1)}, u32[]{:S(2)}, u32[]{:S(2)}) async-start(bf16[8,16,1280]{2,1,0:T(8,128)(2,1)} %bitcast.13), calls=%async_computation | async-start | bytes 655360 | tf_op jit(solution)/shard_map/all_to_all | solution.py:157
  41.6 0.8 reshape_reshape.15
  42.4 1.2 copy.36
  43.6 4.0 %all-to-all-done = bf16[8,16,1280]{2,1,0:T(8,128)(2,1)S(1)} async-done(((bf16[8,16,1280]{2,1,0:T(8,128)(2,1)}), bf16[8,16,1280]{2,1,0:T(8,128)(2,1)S(1)}, u32[]{:S(2)}, u32[]{:S(2)}) %all-to-all-start) | async-done | bytes 327712 | tf_op jit(solution)/shard_map/all_to_all | solution.py:157
  47.6 4.6 %all-to-all-start.7 = ((bf16[128,4,4,80]{0,3,2,1:T(8,128)(2,1)}), bf16[128,4,4,80]{0,3,2,1:T(8,128)(2,1)S(1)}, u32[]{:S(2)}, u32[]{:S(2)}) async-start(bf16[128,4,4,80]{0,3,2,1:T(8,128)(2,1)} %copy.36), calls=%async_computation.7 | async-start | bytes 655360 | tf_op jit(solution)/shard_map/all_to_all | solution.py:169
  52.2 0.8 reshape_reshape.14
  53.0 1.2 copy.34
  54.1 6.3 %all-to-all-done.7 = bf16[128,4,4,80]{0,3,2,1:T(8,128)(2,1)S(1)} async-done(((bf16[128,4,4,80]{0,3,2,1:T(8,128)(2,1)}), bf16[128,4,4,80]{0,3,2,1:T(8,128)(2,1)S(1)}, u32[]{:S(2)}, u32[]{:S(2)}) %all-to-all-start.7) | async-done | bytes 327712 | tf_op jit(solution)/shard_map/all_to_all | solution.py:169
  60.4 3.8 %all-to-all-start.5 = ((bf16[128,4,4,80]{0,3,2,1:T(8,128)(2,1)}), bf16[128,4,4,80]{0,3,2,1:T(8,128)(2,1)S(1)}, u32[]{:S(2)}, u32[]{:S(2)}) async-start(bf16[128,4,4,80]{0,3,2,1:T(8,128)(2,1)} %copy.34), calls=%async_computation.5 | async-start | bytes 655360 | tf_op jit(solution)/shard_map/all_to_all | solution.py:170
  64.2 0.8 reshape_reshape.13
  65.0 1.2 copy.32
  66.2 4.2 %all-to-all-done.5 = bf16[128,4,4,80]{0,3,2,1:T(8,128)(2,1)S(1)} async-done(((bf16[128,4,4,80]{0,3,2,1:T(8,128)(2,1)}), bf16[128,4,4,80]{0,3,2,1:T(8,128)(2,1)S(1)}, u32[]{:S(2)}, u32[]{:S(2)}) %all-to-all-start.5) | async-done | bytes 327712 | tf_op jit(solution)/shard_map/all_to_all | solution.py:170
  70.4 5.4 %all-to-all-start.3 = ((bf16[128,4,4,80]{0,3,2,1:T(8,128)(2,1)}), bf16[128,4,4,80]{0,3,2,1:T(8,128)(2,1)S(1)}, u32[]{:S(2)}, u32[]{:S(2)}) async-start(bf16[128,4,4,80]{0,3,2,1:T(8,128)(2,1)} %copy.32), calls=%async_computation.3 | async-start | bytes 655360 | tf_op jit(solution)/shard_map/all_to_all | solution.py:168
  75.8 0.8 reshape_reshape.12
  76.6 1.2 copy.30
  77.8 4.2 %all-to-all-done.3 = bf16[128,4,4,80]{0,3,2,1:T(8,128)(2,1)S(1)} async-done(((bf16[128,4,4,80]{0,3,2,1:T(8,128)(2,1)}), bf16[128,4,4,80]{0,3,2,1:T(8,128)(2,1)S(1)}, u32[]{:S(2)}, u32[]{:S(2)}) %all-to-all-start.3) | async-done | bytes 327712 | tf_op jit(solution)/shard_map/all_to_all | solution.py:168
  82.0 3.5 %all-to-all-start.1 = ((bf16[128,4,4,80]{0,3,2,1:T(8,128)(2,1)}), bf16[128,4,4,80]{0,3,2,1:T(8,128)(2,1)S(1)}, u32[]{:S(2)}, u32[]{:S(2)}) async-start(bf16[128,4,4,80]{0,3,2,1:T(8,128)(2,1)} %copy.30), calls=%async_computation.1 | async-start | bytes 655360 | tf_op jit(solution)/shard_map/all_to_all | solution.py:167
  85.4 0.6 fusion.18
  88.5 3.0 %all-to-all-done.1 = bf16[128,4,4,80]{0,3,2,1:T(8,128)(2,1)S(1)} async-done(((bf16[128,4,4,80]{0,3,2,1:T(8,128)(2,1)}), bf16[128,4,4,80]{0,3,2,1:T(8,128)(2,1)S(1)}, u32[]{:S(2)}, u32[]{:S(2)}) %all-to-all-start.1) | async-done | bytes 327712 | tf_op jit(solution)/shard_map/all_to_all | solution.py:167
  91.9 2.2 %conditional.3 = ((f32[4,512,1]{1,0,2:T(4,128)S(1)}, f32[4,512,1]{1,0,2:T(4,128)S(1)})) conditional(s32[]{:T(128)} %bitcast.11, (f32[4,512,1]{1,0,2:T(4,128)S(1)}, f32[4,512,1]{1,0,2:T(4,128)S(1)}) %tuple.47, (s32[512]{0:T(512)S(1)}, bf16[512,4,80]{0,2,1:T(8,128)(2,1)S(1)}, bf16[512,4,80]{0,2,1:T(8,128)(2,1)S(1)}, f32[4,512,1]{1,0,2:T(4,128)S(1)}, ...), branch_computations={%region_0.1_spmd, %region_1.4_spmd} | conditional | flops 175378432 | bytes 9938968 | solution.py:73
  92.2 1.0 fusion
  93.2 0.9 exponential_reduce_fusion
  94.2 2.6 %conditional.4 = (f32[512,4,80]{0,2,1:T(8,128)S(1)}) conditional(s32[]{:T(128)} %bitcast.11, f32[512,4,80]{0,2,1:T(8,128)S(1)} %broadcast.97, (s32[512]{0:T(512)S(1)}, bf16[512,4,80]{0,2,1:T(8,128)(2,1)S(1)}, bf16[512,4,80]{0,2,1:T(8,128)(2,1)S(1)}, f32[4,512,1]{1,0,2:T(4,128)S(1)}, f32[4,512,1]{1,0,2:T(4,128)S(1)}, ...), branch_computations={%region_4.5_spmd, %region_5.6_spmd} | conditional | flops 341213184 | bytes 2836488 | solution.py:96
  94.6 2.2 %fusion.3 = f32[512,4,80]{0,2,1:T(8,128)S(1)} fusion(f32[512,4,80]{0,2,1:T(8,128)S(1)} %get-tuple-element.279, bf16[512,4,80]{0,2,1:T(8,128)(2,1)S(1)} %get-tuple-element.285, bf16[512,4,80]{0,2,1:T(8,128)(2,1)S(1)} %get-tuple-element.281, bf16[512,4,80]{0,2,1:T(8,128)(2,1)S(1)} %get-tuple-element.282, f32[4,512]{1,0:T(4,128)S(1)} %bitcast.111, ...), kind=kOutput, calls=%fused_computation.17 | convolution fusion | flops 340951040 | bytes 2572288 | tf_op jit(solution)/shard_map/while/body/eval_jaxpr/while/body/eval_jaxpr/cond/branch_1_fun/hqk,khd->qhd/dot_general | solution.py:89
  96.9 5.3 %conditional.5 = (f32[512,4,80]{0,2,1:T(8,128)S(1)}, f32[512,4,80]{0,2,1:T(8,128)S(1)}, f32[512,4,80]{0,2,1:T(8,128)S(1)}) conditional(s32[]{:T(128)} %bitcast.11, f32[512,4,80]{0,2,1:T(8,128)S(1)} %broadcast.97, (s32[512]{0:T(512)S(1)}, bf16[512,4,80]{0,2,1:T(8,128)(2,1)S(1)}, bf16[512,4,80]{0,2,1:T(8,128)(2,1)S(1)}, f32[4,512,1]{1,0,2:T(4,128)S(1)}, ...), branch_computations={%region_7.8_spmd, %region_8.9_spmd} | conditional | flops 849051648 | bytes 28272720 | solution.py:129
  97.2 0.5 copy-done.4
  97.6 1.5 exponential_divide_fusion
  99.2 0.5 fusion.11
  100.1 0.8 multiply_convert_fusion
  101.0 0.5 fusion.14
  101.4 0.8 fusion.15
  102.3 1.1 copy.44
  103.4 3.5 %all-to-all-start.8 = ((bf16[512,1,4,80]{3,2,1,0:T(4,128)(2,1)}), bf16[512,1,4,80]{3,2,1,0:T(4,128)(2,1)S(1)}, u32[]{:S(2)}, u32[]{:S(2)}) async-start(bf16[512,1,4,80]{3,2,1,0:T(4,128)(2,1)} %bitcast.26), calls=%async_computation.8 | async-start | bytes 1048576 | tf_op jit(solution)/shard_map/all_to_all | solution.py:177
  106.9 1.1 copy.45
  108.0 8.0 %all-to-all-done.8 = bf16[512,1,4,80]{3,2,1,0:T(4,128)(2,1)S(1)} async-done(((bf16[512,1,4,80]{3,2,1,0:T(4,128)(2,1)}), bf16[512,1,4,80]{3,2,1,0:T(4,128)(2,1)S(1)}, u32[]{:S(2)}, u32[]{:S(2)}) %all-to-all-start.8) | async-done | bytes 327712 | tf_op jit(solution)/shard_map/all_to_all | solution.py:177
  116.0 3.5 %all-to-all-start.10 = ((bf16[512,1,4,80]{3,2,1,0:T(4,128)(2,1)}), bf16[512,1,4,80]{3,2,1,0:T(4,128)(2,1)S(1)}, u32[]{:S(2)}, u32[]{:S(2)}) async-start(bf16[512,1,4,80]{3,2,1,0:T(4,128)(2,1)} %bitcast.30), calls=%async_computation.10 | async-start | bytes 1048576 | tf_op jit(solution)/shard_map/all_to_all | solution.py:178
  119.5 1.1 copy.46
  120.6 8.0 %all-to-all-done.10 = bf16[512,1,4,80]{3,2,1,0:T(4,128)(2,1)S(1)} async-done(((bf16[512,1,4,80]{3,2,1,0:T(4,128)(2,1)}), bf16[512,1,4,80]{3,2,1,0:T(4,128)(2,1)S(1)}, u32[]{:S(2)}, u32[]{:S(2)}) %all-to-all-start.10) | async-done | bytes 327712 | tf_op jit(solution)/shard_map/all_to_all | solution.py:178
  128.6 3.5 %all-to-all-start.12 = ((bf16[512,1,4,80]{3,2,1,0:T(4,128)(2,1)}), bf16[512,1,4,80]{3,2,1,0:T(4,128)(2,1)S(1)}, u32[]{:S(2)}, u32[]{:S(2)}) async-start(bf16[512,1,4,80]{3,2,1,0:T(4,128)(2,1)} %bitcast.34), calls=%async_computation.12 | async-start | bytes 1048576 | tf_op jit(solution)/shard_map/all_to_all | solution.py:181
  132.2 1.3 all_to_all.148
  133.5 8.0 %all-to-all-done.12 = bf16[512,1,4,80]{3,2,1,0:T(4,128)(2,1)S(1)} async-done(((bf16[512,1,4,80]{3,2,1,0:T(4,128)(2,1)}), bf16[512,1,4,80]{3,2,1,0:T(4,128)(2,1)S(1)}, u32[]{:S(2)}, u32[]{:S(2)}) %all-to-all-start.12) | async-done | bytes 327712 | tf_op jit(solution)/shard_map/all_to_all | solution.py:181
  141.5 12.4 %all-to-all-start.9 = ((bf16[8,16,1280]{2,1,0:T(8,128)(2,1)}), bf16[8,16,1280]{2,1,0:T(8,128)(2,1)S(1)}, u32[]{:S(2)}, u32[]{:S(2)}) async-start(bf16[8,16,1280]{2,1,0:T(8,128)(2,1)} %all_to_all.148), calls=%async_computation.9 | async-start | bytes 655360 | tf_op jit(solution)/shard_map/all_to_all | solution.py:191
  154.1 1.3 all_to_all.154
  155.4 4.5 %all-to-all-done.9 = bf16[8,16,1280]{2,1,0:T(8,128)(2,1)S(1)} async-done(((bf16[8,16,1280]{2,1,0:T(8,128)(2,1)}), bf16[8,16,1280]{2,1,0:T(8,128)(2,1)S(1)}, u32[]{:S(2)}, u32[]{:S(2)}) %all-to-all-start.9) | async-done | bytes 327712 | tf_op jit(solution)/shard_map/all_to_all | solution.py:191
  159.9 5.0 %all-to-all-start.11 = ((bf16[8,16,1280]{2,1,0:T(8,128)(2,1)}), bf16[8,16,1280]{2,1,0:T(8,128)(2,1)S(1)}, u32[]{:S(2)}, u32[]{:S(2)}) async-start(bf16[8,16,1280]{2,1,0:T(8,128)(2,1)} %all_to_all.154), calls=%async_computation.11 | async-start | bytes 655360 | tf_op jit(solution)/shard_map/all_to_all | solution.py:192
  164.9 1.0 scatter_custom_fusion
  166.1 1.3 all_to_all.160
  167.4 3.6 %all-to-all-done.11 = bf16[8,16,1280]{2,1,0:T(8,128)(2,1)S(1)} async-done(((bf16[8,16,1280]{2,1,0:T(8,128)(2,1)}), bf16[8,16,1280]{2,1,0:T(8,128)(2,1)S(1)}, u32[]{:S(2)}, u32[]{:S(2)}) %all-to-all-start.11) | async-done | bytes 327712 | tf_op jit(solution)/shard_map/all_to_all | solution.py:192
  170.9 5.0 %all-to-all-start.13 = ((bf16[8,16,1280]{2,1,0:T(8,128)(2,1)}), bf16[8,16,1280]{2,1,0:T(8,128)(2,1)S(1)}, u32[]{:S(2)}, u32[]{:S(2)}) async-start(bf16[8,16,1280]{2,1,0:T(8,128)(2,1)} %all_to_all.160), calls=%async_computation.13 | async-start | bytes 655360 | tf_op jit(solution)/shard_map/all_to_all | solution.py:193
  175.9 1.6 gather_fusion.4
  177.6 1.6 gather_fusion.5
  179.2 2.8 %all-to-all-done.13 = bf16[8,16,1280]{2,1,0:T(8,128)(2,1)S(1)} async-done(((bf16[8,16,1280]{2,1,0:T(8,128)(2,1)}), bf16[8,16,1280]{2,1,0:T(8,128)(2,1)S(1)}, u32[]{:S(2)}, u32[]{:S(2)}) %all-to-all-start.13) | async-done | bytes 327712 | tf_op jit(solution)/shard_map/all_to_all | solution.py:193
  181.9 1.6 gather_fusion.6
  (41 shorter events, 3.7 us)
Async XLA Ops:
  0.6 1.0 copy-start
  0.6 7.9 %copy-start.1 = (bf16[128,1280]{1,0:T(8,128)(2,1)S(1)}, bf16[128,1280]{1,0:T(8,128)(2,1)}, u32[]{:S(2)}) copy-start(bf16[128,1280]{1,0:T(8,128)(2,1)} %param.15) | copy-start | bytes 983044
  0.7 18.9 %copy-start.2 = (bf16[128,1280]{1,0:T(8,128)(2,1)S(1)}, bf16[128,1280]{1,0:T(8,128)(2,1)}, u32[]{:S(2)}) copy-start(bf16[128,1280]{1,0:T(8,128)(2,1)} %param.13) | copy-start | bytes 983044
  3.2 27.3 %copy-start.3 = (bf16[128,1280]{1,0:T(8,128)(2,1)S(1)}, bf16[128,1280]{1,0:T(8,128)(2,1)}, u32[]{:S(2)}) copy-start(bf16[128,1280]{1,0:T(8,128)(2,1)} %param.12) | copy-start | bytes 983044
  3.2 11.3 %all-to-all-start.6 = ((bf16[8,16,1280]{2,1,0:T(8,128)(2,1)}), bf16[8,16,1280]{2,1,0:T(8,128)(2,1)S(1)}, u32[]{:S(2)}, u32[]{:S(2)}) async-start(bf16[8,16,1280]{2,1,0:T(8,128)(2,1)} %bitcast.22), calls=%async_computation.6 | async-start | bytes 655360 | tf_op jit(solution)/shard_map/all_to_all | solution.py:159
  14.5 11.0 %all-to-all-start.4 = ((bf16[8,16,1280]{2,1,0:T(8,128)(2,1)}), bf16[8,16,1280]{2,1,0:T(8,128)(2,1)S(1)}, u32[]{:S(2)}, u32[]{:S(2)}) async-start(bf16[8,16,1280]{2,1,0:T(8,128)(2,1)} %bitcast.19), calls=%async_computation.4 | async-start | bytes 655360 | tf_op jit(solution)/shard_map/all_to_all | solution.py:160
  25.6 11.0 %all-to-all-start.2 = ((bf16[8,16,1280]{2,1,0:T(8,128)(2,1)}), bf16[8,16,1280]{2,1,0:T(8,128)(2,1)S(1)}, u32[]{:S(2)}, u32[]{:S(2)}) async-start(bf16[8,16,1280]{2,1,0:T(8,128)(2,1)} %bitcast.16), calls=%async_computation.2 | async-start | bytes 655360 | tf_op jit(solution)/shard_map/all_to_all | solution.py:158
  36.6 11.0 %all-to-all-start = ((bf16[8,16,1280]{2,1,0:T(8,128)(2,1)}), bf16[8,16,1280]{2,1,0:T(8,128)(2,1)S(1)}, u32[]{:S(2)}, u32[]{:S(2)}) async-start(bf16[8,16,1280]{2,1,0:T(8,128)(2,1)} %bitcast.13), calls=%async_computation | async-start | bytes 655360 | tf_op jit(solution)/shard_map/all_to_all | solution.py:157
  42.4 43.1 %copy-start.6 = (s32[1,512]{1,0:T(1,128)S(1)}, s32[1,512]{1,0:T(1,128)}, u32[]{:S(2)}) copy-start(s32[1,512]{1,0:T(1,128)} %param.17) | copy-start | bytes 6148
  47.6 12.9 %all-to-all-start.7 = ((bf16[128,4,4,80]{0,3,2,1:T(8,128)(2,1)}), bf16[128,4,4,80]{0,3,2,1:T(8,128)(2,1)S(1)}, u32[]{:S(2)}, u32[]{:S(2)}) async-start(bf16[128,4,4,80]{0,3,2,1:T(8,128)(2,1)} %copy.36), calls=%async_computation.7 | async-start | bytes 655360 | tf_op jit(solution)/shard_map/all_to_all | solution.py:169
  60.4 10.0 %all-to-all-start.5 = ((bf16[128,4,4,80]{0,3,2,1:T(8,128)(2,1)}), bf16[128,4,4,80]{0,3,2,1:T(8,128)(2,1)S(1)}, u32[]{:S(2)}, u32[]{:S(2)}) async-start(bf16[128,4,4,80]{0,3,2,1:T(8,128)(2,1)} %copy.34), calls=%async_computation.5 | async-start | bytes 655360 | tf_op jit(solution)/shard_map/all_to_all | solution.py:170
  70.4 11.6 %all-to-all-start.3 = ((bf16[128,4,4,80]{0,3,2,1:T(8,128)(2,1)}), bf16[128,4,4,80]{0,3,2,1:T(8,128)(2,1)S(1)}, u32[]{:S(2)}, u32[]{:S(2)}) async-start(bf16[128,4,4,80]{0,3,2,1:T(8,128)(2,1)} %copy.32), calls=%async_computation.3 | async-start | bytes 655360 | tf_op jit(solution)/shard_map/all_to_all | solution.py:168
  82.0 9.6 %all-to-all-start.1 = ((bf16[128,4,4,80]{0,3,2,1:T(8,128)(2,1)}), bf16[128,4,4,80]{0,3,2,1:T(8,128)(2,1)S(1)}, u32[]{:S(2)}, u32[]{:S(2)}) async-start(bf16[128,4,4,80]{0,3,2,1:T(8,128)(2,1)} %copy.30), calls=%async_computation.1 | async-start | bytes 655360 | tf_op jit(solution)/shard_map/all_to_all | solution.py:167
  96.9 0.7 copy-start.4
  99.2 1.0 copy-start.5
  103.4 12.6 %all-to-all-start.8 = ((bf16[512,1,4,80]{3,2,1,0:T(4,128)(2,1)}), bf16[512,1,4,80]{3,2,1,0:T(4,128)(2,1)S(1)}, u32[]{:S(2)}, u32[]{:S(2)}) async-start(bf16[512,1,4,80]{3,2,1,0:T(4,128)(2,1)} %bitcast.26), calls=%async_computation.8 | async-start | bytes 1048576 | tf_op jit(solution)/shard_map/all_to_all | solution.py:177
  116.0 12.6 %all-to-all-start.10 = ((bf16[512,1,4,80]{3,2,1,0:T(4,128)(2,1)}), bf16[512,1,4,80]{3,2,1,0:T(4,128)(2,1)S(1)}, u32[]{:S(2)}, u32[]{:S(2)}) async-start(bf16[512,1,4,80]{3,2,1,0:T(4,128)(2,1)} %bitcast.30), calls=%async_computation.10 | async-start | bytes 1048576 | tf_op jit(solution)/shard_map/all_to_all | solution.py:178
  128.6 12.9 %all-to-all-start.12 = ((bf16[512,1,4,80]{3,2,1,0:T(4,128)(2,1)}), bf16[512,1,4,80]{3,2,1,0:T(4,128)(2,1)S(1)}, u32[]{:S(2)}, u32[]{:S(2)}) async-start(bf16[512,1,4,80]{3,2,1,0:T(4,128)(2,1)} %bitcast.34), calls=%async_computation.12 | async-start | bytes 1048576 | tf_op jit(solution)/shard_map/all_to_all | solution.py:181
  141.5 18.4 %all-to-all-start.9 = ((bf16[8,16,1280]{2,1,0:T(8,128)(2,1)}), bf16[8,16,1280]{2,1,0:T(8,128)(2,1)S(1)}, u32[]{:S(2)}, u32[]{:S(2)}) async-start(bf16[8,16,1280]{2,1,0:T(8,128)(2,1)} %all_to_all.148), calls=%async_computation.9 | async-start | bytes 655360 | tf_op jit(solution)/shard_map/all_to_all | solution.py:191
  159.9 11.0 %all-to-all-start.11 = ((bf16[8,16,1280]{2,1,0:T(8,128)(2,1)}), bf16[8,16,1280]{2,1,0:T(8,128)(2,1)S(1)}, u32[]{:S(2)}, u32[]{:S(2)}) async-start(bf16[8,16,1280]{2,1,0:T(8,128)(2,1)} %all_to_all.154), calls=%async_computation.11 | async-start | bytes 655360 | tf_op jit(solution)/shard_map/all_to_all | solution.py:192
  170.9 11.0 %all-to-all-start.13 = ((bf16[8,16,1280]{2,1,0:T(8,128)(2,1)}), bf16[8,16,1280]{2,1,0:T(8,128)(2,1)S(1)}, u32[]{:S(2)}, u32[]{:S(2)}) async-start(bf16[8,16,1280]{2,1,0:T(8,128)(2,1)} %all_to_all.160), calls=%async_computation.13 | async-start | bytes 655360 | tf_op jit(solution)/shard_map/all_to_all | solution.py:193
where the time goes:
time: 187 us; the launch traced here: 184 us
  starting transfers between devices  70.5 us (38%)
  waiting for transfers between devices  69.7 us (37%)
  local copies, waits for them, and re-layouts  31 us (17%)
  matrix products  7.26 us (4%)
  other arithmetic  2.57 us (1%)
  between operations  2.2 us (1%)
    all_to_all x1, starting transfers between devices, on_device(): lax.all_to_all(flat[0], 'dp', split_axis=0, concat_axis=0, tiled=True)  12.4 us
    all_to_all x1, waiting for transfers between devices, on_device(): lax.all_to_all(grads[0][:, None], 'seq', split_axis=0, concat_axis=1, til...  8.02 us
    all_to_all x1, waiting for transfers between devices, on_device(): lax.all_to_all(grads[2].astype(jnp.bfloat16)[:, None], 'seq', split_axis=...  7.99 us
    all_to_all x1, waiting for transfers between devices, on_device(): lax.all_to_all(grads[1].astype(jnp.bfloat16)[:, None], 'seq', split_axis=...  7.97 us
    another operation x8, local copies, waits for them, and re-layouts, on_device(): item.reshape(rows, seq_devs, own_heads, HD)  7.82 us
    all_to_all x1, waiting for transfers between devices, on_device(): lax.all_to_all(split_form[2], 'seq', split_axis=1, concat_axis=0, tiled=T...  6.31 us
    all_to_all x1, starting transfers between devices, on_device(): lax.all_to_all(split_form[1], 'seq', split_axis=1, concat_axis=0, tiled=T...  5.4 us
    all_to_all x1, starting transfers between devices, on_device(): lax.all_to_all(permuted[2], 'dp', split_axis=0, concat_axis=0, tiled=True)  5.35 us
  transfers between devices with their start and end apart: 14, of which 14 were waited for; matrix products, arithmetic and copies ran while one was open for 12% of the time, Pallas kernels for 0%

commit v1 on v0

v1 whole, which is shorter than its diff:
```python
import functools
import math

import jax
import jax.numpy as jnp
from jax import lax
from jax.experimental import pallas as pl
from jax.experimental.pallas import tpu as pltpu
from jax.sharding import PartitionSpec as P

HD = 80
NEG_FILL = -1e30
VMEM_LIMIT = 48 * 1024 * 1024
NT = (((1,), (1,)), ((), ()))
LANES = 128


def in_vmem(count):
    return [pl.BlockSpec(memory_space=pltpu.VMEM)] * count


def params():
    return pltpu.CompilerParams(vmem_limit_bytes=VMEM_LIMIT)


def bf16(*shape):
    return jax.ShapeDtypeStruct(shape, jnp.bfloat16)


def one_hot_columns(order_ref, rows):
    source = lax.broadcasted_iota(jnp.int32, (rows, rows), 0)
    return (source == order_ref[...]).astype(jnp.bfloat16)


def segment_marks(seg_ref, seq_devs, slice_rows):
    rows = seg_ref.shape[1]
    cut = jnp.sum(jnp.where(seg_ref[...] == 0, 1, 0))
    place = lax.broadcasted_iota(jnp.int32, (rows, 2), 0)
    device, part = (place // slice_rows) % seq_devs, place // (slice_rows * seq_devs)
    row = device * (rows // seq_devs) + part * slice_rows + place % slice_rows
    first = jnp.where(row < cut, 1.0, 0.0)
    own = jnp.where(lax.broadcasted_iota(jnp.int32, (rows, 2), 1) == 0, first, 1.0 - first)
    blank = jnp.zeros((rows, LANES - 2), jnp.float32)
    return tuple(
        jnp.concatenate([blank[:, :HD], mark, blank[:, HD:]], axis=1).astype(jnp.bfloat16)
        for mark in (own, (1.0 - own) * NEG_FILL)
    )


def chunk_rows(total):
    step = min(total, 32)
    return [slice(start, start + step) for start in range(0, total, step)]


def eights(chunk, reduce):
    return reduce(chunk.reshape(chunk.shape[0] // 8, 8, chunk.shape[1]), axis=0)


def score_passes(score_ref, dprob_ref, at, probs_ref, dscores_ref):
    scale = math.log2(math.e) / math.sqrt(HD)
    chunks = chunk_rows(score_ref.shape[0])
    top = functools.reduce(jnp.maximum, [eights(score_ref[rows], jnp.max) for rows in chunks])
    top = jnp.max(top, axis=0, keepdims=True) * scale
    total = jnp.zeros((8, score_ref.shape[1]), jnp.float32)
    delta = total
    for rows in chunks:
        shifted = jnp.exp2(score_ref[rows] * scale - top)
        score_ref[rows] = shifted
        total += eights(shifted, jnp.sum)
        delta += eights(shifted * dprob_ref[rows], jnp.sum)
    weight = 1.0 / jnp.sum(total, axis=0, keepdims=True)
    delta = jnp.sum(delta, axis=0, keepdims=True) * weight
    for rows in chunks:
        probs = score_ref[rows] * weight
        probs_ref[rows, at] = probs.astype(jnp.bfloat16)
        dscores_ref[rows, at] = (probs * (dprob_ref[rows] - delta)).astype(jnp.bfloat16)


def pack_kernel(folds, seg_ref, order_ref, *refs):
    inputs, (out_ref, query_mark, key_mark, hot_ref), (landed, seg_vmem, order_vmem, sems) = refs[:4], refs[4:8], refs[8:]
    rows, columns = inputs[0].shape
    seq_devs, slice_rows = out_ref.shape[1:3]
    own = columns // seq_devs
    copies = [
        pltpu.make_async_copy(order_ref, order_vmem, sems.at[4]),
        pltpu.make_async_copy(seg_ref, seg_vmem, sems.at[5]),
    ]
    copies += [pltpu.make_async_copy(ref, landed.at[index], sems.at[index]) for index, ref in enumerate(inputs)]
    for copy in copies:
        copy.start()
    copies[0].wait()
    columns_hot = one_hot_columns(order_vmem, rows)
    hot = columns_hot.T
    if folds > 1:
        places = columns_hot.astype(jnp.float32).T.reshape(rows // slice_rows, folds, slice_rows // folds, rows)
        places = [places[:, fold].reshape(rows // folds, rows) for fold in range(folds)]
        columns_hot = jnp.concatenate(places, axis=0).T.astype(jnp.bfloat16)
    hot_ref[...] = columns_hot
    copies[1].wait()
    query_mark[...], key_mark[...] = segment_marks(seg_vmem, seq_devs, slice_rows)
    for index in range(4):
        copies[2 + index].wait()
        permuted = jnp.dot(hot, landed[index], preferred_element_type=jnp.float32).astype(jnp.bfloat16)
        for peer in range(seq_devs):
            columns_of = permuted[:, peer * own : (peer + 1) * own]
            out_ref[:, peer, :, index * own : (index + 1) * own] = columns_of.reshape(-1, slice_rows, own)


def attention_kernel(heads, folds, slice_rows, query_mark, key_mark, x_ref, out_ref, scores, dprobs, probs, dscores):
    rows, span = scores.shape[1:]
    width, part = 3 * heads * HD, slice_rows // folds
    inv_root = 1.0 / math.sqrt(HD)

    def piece(array, head):
        return x_ref[:, (array * heads + head) * HD : (array * heads + head + 1) * HD]

    def products(step):
        head, at = steps[step]
        if head not in held:
            held[head] = tuple(piece(array, head) for array in range(4))
        query, key, value, grad = held[head]
        marked_query = jnp.concatenate([query[at], query_mark[at, HD:]], axis=1)
        marked_key = jnp.concatenate([key, key_mark[:, HD:]], axis=1)
        scores[step % 2] = lax.dot_general(marked_key, marked_query, NT, preferred_element_type=jnp.float32)
        dprobs[step % 2] = lax.dot_general(value, grad[at], NT, preferred_element_type=jnp.float32)

    def store(array, head, value):
        start = (array * heads + head) * HD
        split = value.reshape(rows // slice_rows, folds, part, HD)
        for fold in range(folds):
            out_ref[:, fold * width + start : fold * width + start + HD] = (
                split[:, fold].reshape(rows // folds, HD).astype(jnp.bfloat16)
            )

    held = {}
    steps = [(head, slice(start, start + span)) for head in range(heads) for start in range(0, rows, span)]
    products(0)
    for step, (head, at) in enumerate(steps):
        if step + 1 < len(steps):
            products(step + 1)
        slot = head % probs.shape[0]
        score_passes(scores.at[step % 2], dprobs.at[step % 2], at, probs.at[slot], dscores.at[slot])
        if at.stop == rows:
            query, key, _, grad = held[head]
            grad_q = jnp.dot(key.T, dscores[slot], preferred_element_type=jnp.float32)
            store(0, head, grad_q.T * inv_root)
            store(1, head, jnp.dot(dscores[slot], query, preferred_element_type=jnp.float32) * inv_root)
            store(2, head, jnp.dot(probs[slot], grad, preferred_element_type=jnp.float32))


def unpack_kernel(folds, hot_ref, packed_ref, *outs):
    rows, columns = outs[0].shape
    seq_devs = packed_ref.shape[1]
    own = columns // seq_devs
    hot = hot_ref[...]
    for index, ref in enumerate(outs):
        whole = []
        for fold in range(folds):
            start = (fold * 3 + index) * own
            pieces = [
                packed_ref[:, peer, :, start : start + own].reshape(rows // folds, own) for peer in range(seq_devs)
            ]
            whole.append(jnp.concatenate(pieces, axis=1))
        ref[...] = jnp.dot(
            hot, jnp.concatenate(whole, axis=0), preferred_element_type=jnp.float32
        ).astype(jnp.bfloat16)


def on_device(queries, key_states, value_states, out_grads, row_order, segment_ids):
    rows, columns = queries.shape
    dp_devs, seq_devs = lax.axis_size("dp"), lax.axis_size("seq")
    own = columns // seq_devs
    heads = own // HD
    peers = dp_devs * seq_devs
    slice_rows = rows // dp_devs
    group_rows = rows * seq_devs
    span = min(group_rows, 512)
    folds = 2 if slice_rows % 16 == 0 and 3 * own % 128 else 1
    order = row_order.reshape(1, rows)
    arrays = (segment_ids, order, queries, key_states, value_states, out_grads)

    packed, query_mark, key_mark, hot = pl.pallas_call(
        functools.partial(pack_kernel, folds),
        out_shape=[
            bf16(dp_devs, seq_devs, slice_rows, 4 * own),
            bf16(group_rows, LANES),
            bf16(group_rows, LANES),
            bf16(rows, rows),
        ],
        in_specs=[pl.BlockSpec(memory_space=pltpu.HBM)] * 6,
        out_specs=in_vmem(4),
        scratch_shapes=[
            pltpu.VMEM((4, rows, columns), jnp.bfloat16),
            pltpu.VMEM((1, group_rows), jnp.int32),
            pltpu.VMEM((1, rows), jnp.int32),
            pltpu.SemaphoreType.DMA((6,)),
        ],
        compiler_params=params(),
        name="pack",
    )(*(pltpu.with_memory_space_constraint(array, pltpu.HBM) for array in arrays))
    moved = lax.all_to_all(
        packed.reshape(peers, slice_rows, 4 * own), ("dp", "seq"), split_axis=0, concat_axis=0, tiled=True
    )
    grads = pl.pallas_call(
        functools.partial(attention_kernel, heads, folds, slice_rows),
        out_shape=bf16(group_rows // folds, folds * 3 * own),
        in_specs=in_vmem(3),
        out_specs=in_vmem(1)[0],
        scratch_shapes=[
            pltpu.VMEM((2, group_rows, span), jnp.float32),
            pltpu.VMEM((2, group_rows, span), jnp.float32),
            pltpu.VMEM((min(heads, 2), group_rows, group_rows), jnp.bfloat16),
            pltpu.VMEM((min(heads, 2), group_rows, group_rows), jnp.bfloat16),
        ],
        compiler_params=params(),
        name="attention",
    )(query_mark, key_mark, moved.reshape(group_rows, 4 * own))
    returned = lax.all_to_all(
        grads.reshape(peers, slice_rows // folds, folds * 3 * own),
        ("dp", "seq"),
        split_axis=0,
        concat_axis=0,
        tiled=True,
    )
    return pl.pallas_call(
        functools.partial(unpack_kernel, folds),
        out_shape=[bf16(rows, columns)] * 3,
        in_specs=in_vmem(2),
        out_specs=in_vmem(3),
        compiler_params=params(),
        name="unpack",
    )(hot, returned.reshape(dp_devs, seq_devs, slice_rows // folds, folds * 3 * own))


def solution(mesh):
    rows = P(("dp", "seq"), None)
    return jax.shard_map(
        on_device,
        mesh=mesh,
        in_specs=(rows, rows, rows, rows, P(("dp", "seq")), P("dp", None)),
        out_specs=(rows, rows, rows),
        check_vma=False,
    )
```

time: 187 us -> 75.6 us (0.40); the launches traced: 184 us -> 75.4 us
  starting transfers between devices: 70.5 us -> 0 us
  waiting for transfers between devices: 69.7 us -> 0 us
  blocking collectives: 0 us -> 67.1 us
  local copies, waits for them, and re-layouts: 31 us -> 0 us
  Pallas kernels: 0 us -> 7.67 us
  matrix products: 7.26 us -> 0 us
  other arithmetic: 2.57 us -> 0 us
    all_to_all x14 -> x0, starting transfers between devices: 70.5 us -> none  [the longest x1 12.4 us: on_device(): lax.all_to_all(flat[0], 'dp', split_axis=0, concat_axis=0, tiled=True)]
    all_to_all x14 -> x0, waiting for transfers between devices: 69.7 us -> none  [the longest x1 8.02 us: on_device(): lax.all_to_all(grads[0][:, None], 'seq', split_axis=0, concat_axis=1, til...]
    all_to_all x0 -> x2, blocking collectives: none -> 67.1 us  [the longest x1 39.7 us: on_device(): lax.all_to_all(packed.reshape(peers, slice_rows, 4 * own), ('dp', 'seq'),...]
    gather x7 -> x0, local copies, waits for them, and re-layouts: 11.3 us -> none  [the longest x3 4.84 us: on_device(): return (returned[0][inverse], returned[1][inverse], returned[2][inverse])]
    another operation x11 -> x0, local copies, waits for them, and re-layouts: 7.89 us -> none  [the longest x8 7.82 us: on_device(): item.reshape(rows, seq_devs, own_heads, HD)]
    pallas_call x0 -> x3, Pallas kernels: none -> 7.67 us  [the longest x1 4.01 us: on_device(): pl.pallas_call(functools.partial(attention_kernel, heads, folds, slice_ro...]
    dot_general x7 -> x0, matrix products: 7.26 us -> none  [the longest x2 2.48 us: score_block(): jnp.einsum('qhd,khd->hqk', query_block, key_block, preferred_element_type...]
    all_to_all x10 -> x0, local copies, waits for them, and re-layouts: 5.38 us -> none  [the longest x1 1.27 us: on_device(): lax.all_to_all(flat[0], 'dp', split_axis=0, concat_axis=0, tiled=True)]
  transfers between devices with their start and end apart: 14 -> 0, of which waited for: 14 -> 0; matrix products, arithmetic and copies ran while one was open for 12% -> 0% of each run, Pallas kernels for 0% -> 0%
where the time goes in v1:
time: 75.6 us; the launch traced here: 75.4 us
  blocking collectives  67.1 us (89%)
  Pallas kernels  7.67 us (10%)
    all_to_all x1, blocking collectives, on_device(): lax.all_to_all(packed.reshape(peers, slice_rows, 4 * own), ('dp', 'seq'),...  39.7 us
    all_to_all x1, blocking collectives, on_device(): lax.all_to_all(grads.reshape(peers, slice_rows // folds, folds * 3 * own)...  27.4 us
    pallas_call x1, Pallas kernels, on_device(): pl.pallas_call(functools.partial(attention_kernel, heads, folds, slice_ro...  4.01 us
    pallas_call x1, Pallas kernels, on_device(): pl.pallas_call(functools.partial(pack_kernel, folds), out_shape=[bf16(dp_...  2.41 us

profile of v1, /device:TPU:1, one launch (start us, length us, event | category | flops | bytes accessed | tf_op | source)
XLA Modules:
  0.0 75.4 jit_solution(3840510870200607913)
XLA Ops:
  0.6 2.4 %pack.1 = (bf16[8,4,16,1280]{3,2,1,0:T(8,128)(2,1)S(1)}, bf16[512,128]{1,0:T(8,128)(2,1)S(1)}, bf16[512,128]{1,0:T(8,128)(2,1)S(1)}, bf16[128,128]{1,0:T(8,128)(2,1)S(1)}) custom-call(s32[1,512]{1,0:T(1,128)} %seg_ref.1, s32[1,128]{1,0:T(1,128)} %bitcast.9, bf16[128,1280]{1,0:T(8,128)(2,1)} %refs_0_.1, bf16[128,1280]{1,0:T(8,128)(2,1)} %refs_1_.1, ...), custom_call_target="tpu_custom_call" | custom-call | tf_op jit(solution)/shard_map/pack/pallas_call | solution.py:182
  3.1 39.7 %all_to_all.10 = bf16[32,16,1280]{2,1,0:T(8,128)(2,1)S(1)} all-to-all(bf16[32,16,1280]{2,1,0:T(8,128)(2,1)S(1)} %bitcast.8), channel_id=1, replica_groups=mesh['dp'=8,'seq'=4] {'dp','seq'}, dimensions={0} | all-to-all | bytes 2621440 | tf_op jit(solution)/shard_map/all_to_all | solution.py:201
  42.8 4.0 %attention.1 = bf16[256,1920]{1,0:T(8,128)(2,1)S(1)} custom-call(bf16[512,128]{1,0:T(8,128)(2,1)S(1)} %get-tuple-element.8.query_mark, bf16[512,128]{1,0:T(8,128)(2,1)S(1)} %get-tuple-element.9.key_mark, bf16[512,1280]{1,0:T(8,128)(2,1)S(1)} %bitcast.5), custom_call_target="tpu_custom_call" | custom-call | tf_op jit(solution)/shard_map/attention/pallas_call | solution.py:204
  46.8 27.4 %all_to_all.11 = bf16[32,8,1920]{2,1,0:T(8,128)(2,1)S(1)} all-to-all(bf16[32,8,1920]{2,1,0:T(8,128)(2,1)S(1)} %bitcast.7), channel_id=1, replica_groups=mesh['dp'=8,'seq'=4] {'dp','seq'}, dimensions={0} | all-to-all | bytes 1966080 | tf_op jit(solution)/shard_map/all_to_all | solution.py:218
  74.1 1.3 %unpack.1 = (bf16[128,1280]{1,0:T(8,128)(2,1)}, bf16[128,1280]{1,0:T(8,128)(2,1)}, bf16[128,1280]{1,0:T(8,128)(2,1)}) custom-call(bf16[128,128]{1,0:T(8,128)(2,1)S(1)} %get-tuple-element.7.hot_ref, bf16[8,4,8,1920]{3,2,1,0:T(8,128)(2,1)S(1)} %bitcast.6), custom_call_target="tpu_custom_call" | custom-call | tf_op jit(solution)/shard_map/unpack/pallas_call | solution.py:225

commit v2 on v1

--- a/solution.py
+++ b/solution.py
@@ -106,7 +106,7 @@
             out_ref[:, peer, :, index * own : (index + 1) * own] = columns_of.reshape(-1, slice_rows, own)
 
 
-def attention_kernel(heads, folds, slice_rows, query_mark, key_mark, x_ref, out_ref, scores, dprobs, probs, dscores):
+def attention_kernel(heads, folds, slice_rows, query_mark, key_mark, x_ref, out_ref, scores, dprobs, probs, dscores, grad_q):
     rows, span = scores.shape[1:]
     width, part = 3 * heads * HD, slice_rows // folds
     inv_root = 1.0 / math.sqrt(HD)
@@ -125,13 +125,16 @@
         dprobs[step % 2] = lax.dot_general(value, grad[at], NT, preferred_element_type=jnp.float32)
 
     def store(array, head, value):
-        start = (array * heads + head) * HD
-        split = value.reshape(rows // slice_rows, folds, part, HD)
+        start, columns = (array * heads + head) * HD, value.shape[1]
+        split = value.reshape(rows // slice_rows, folds, part, columns)
         for fold in range(folds):
-            out_ref[:, fold * width + start : fold * width + start + HD] = (
-                split[:, fold].reshape(rows // folds, HD).astype(jnp.bfloat16)
+            out_ref[:, fold * width + start : fold * width + start + columns] = (
+                split[:, fold].reshape(rows // folds, columns).astype(jnp.bfloat16)
             )
 
+    own = heads * HD
+    first = own // LANES * LANES
+    key_t = x_ref[:, first : -(-2 * own // LANES) * LANES].T[own - first : 2 * own - first]
     held = {}
     steps = [(head, slice(start, start + span)) for head in range(heads) for start in range(0, rows, span)]
     products(0)
@@ -141,11 +144,12 @@
         slot = head % probs.shape[0]
         score_passes(scores.at[step % 2], dprobs.at[step % 2], at, probs.at[slot], dscores.at[slot])
         if at.stop == rows:
-            query, key, _, grad = held[head]
-            grad_q = jnp.dot(key.T, dscores[slot], preferred_element_type=jnp.float32)
-            store(0, head, grad_q.T * inv_root)
+            query, _, _, grad = held[head]
+            lanes = slice(head * HD, (head + 1) * HD)
+            grad_q[lanes, :] = jnp.dot(key_t[lanes], dscores[slot], preferred_element_type=jnp.float32)
             store(1, head, jnp.dot(dscores[slot], query, preferred_element_type=jnp.float32) * inv_root)
             store(2, head, jnp.dot(probs[slot], grad, preferred_element_type=jnp.float32))
+    store(0, 0, grad_q[...].T * inv_root)
 
 
 def unpack_kernel(folds, hot_ref, packed_ref, *outs):
@@ -211,6 +215,7 @@
             pltpu.VMEM((2, group_rows, span), jnp.float32),
             pltpu.VMEM((min(heads, 2), group_rows, group_rows), jnp.bfloat16),
             pltpu.VMEM((min(heads, 2), group_rows, group_rows), jnp.bfloat16),
+            pltpu.VMEM((own, group_rows), jnp.float32),
         ],
         compiler_params=params(),
         name="attention",

time: 75.6 us -> 75.5 us (level)
  no operation moved by 1% of the time
where the time goes in v2:
time: 75.5 us; the launch traced here: 75.4 us
  blocking collectives  67.1 us (89%)
  Pallas kernels  7.62 us (10%)
    all_to_all x1, blocking collectives, on_device(): lax.all_to_all(packed.reshape(peers, slice_rows, 4 * own), ('dp', 'seq'),...  39.7 us
    all_to_all x1, blocking collectives, on_device(): lax.all_to_all(grads.reshape(peers, slice_rows // folds, folds * 3 * own)...  27.4 us
    pallas_call x1, Pallas kernels, on_device(): pl.pallas_call(functools.partial(attention_kernel, heads, folds, slice_ro...  3.95 us
    pallas_call x1, Pallas kernels, on_device(): pl.pallas_call(functools.partial(pack_kernel, folds), out_shape=[bf16(dp_...  2.41 us

profile of v2, /device:TPU:1, one launch (start us, length us, event | category | flops | bytes accessed | tf_op | source)
XLA Modules:
  0.0 75.4 jit_solution(14887643861464612318)
XLA Ops:
  0.6 2.4 %pack.1 = (bf16[8,4,16,1280]{3,2,1,0:T(8,128)(2,1)S(1)}, bf16[512,128]{1,0:T(8,128)(2,1)S(1)}, bf16[512,128]{1,0:T(8,128)(2,1)S(1)}, bf16[128,128]{1,0:T(8,128)(2,1)S(1)}) custom-call(s32[1,512]{1,0:T(1,128)} %seg_ref.1, s32[1,128]{1,0:T(1,128)} %bitcast.9, bf16[128,1280]{1,0:T(8,128)(2,1)} %refs_0_.1, bf16[128,1280]{1,0:T(8,128)(2,1)} %refs_1_.1, ...), custom_call_target="tpu_custom_call" | custom-call | tf_op jit(solution)/shard_map/pack/pallas_call | solution.py:186
  3.1 39.7 %all_to_all.10 = bf16[32,16,1280]{2,1,0:T(8,128)(2,1)S(1)} all-to-all(bf16[32,16,1280]{2,1,0:T(8,128)(2,1)S(1)} %bitcast.8), channel_id=1, replica_groups=mesh['dp'=8,'seq'=4] {'dp','seq'}, dimensions={0} | all-to-all | bytes 2621440 | tf_op jit(solution)/shard_map/all_to_all | solution.py:205
  42.8 4.0 %attention.1 = bf16[256,1920]{1,0:T(8,128)(2,1)S(1)} custom-call(bf16[512,128]{1,0:T(8,128)(2,1)S(1)} %get-tuple-element.8.query_mark, bf16[512,128]{1,0:T(8,128)(2,1)S(1)} %get-tuple-element.9.key_mark, bf16[512,1280]{1,0:T(8,128)(2,1)S(1)} %bitcast.5), custom_call_target="tpu_custom_call" | custom-call | tf_op jit(solution)/shard_map/attention/pallas_call | solution.py:208
  46.7 27.4 %all_to_all.11 = bf16[32,8,1920]{2,1,0:T(8,128)(2,1)S(1)} all-to-all(bf16[32,8,1920]{2,1,0:T(8,128)(2,1)S(1)} %bitcast.7), channel_id=1, replica_groups=mesh['dp'=8,'seq'=4] {'dp','seq'}, dimensions={0} | all-to-all | bytes 1966080 | tf_op jit(solution)/shard_map/all_to_all | solution.py:223
  74.1 1.3 %unpack.1 = (bf16[128,1280]{1,0:T(8,128)(2,1)}, bf16[128,1280]{1,0:T(8,128)(2,1)}, bf16[128,1280]{1,0:T(8,128)(2,1)}) custom-call(bf16[128,128]{1,0:T(8,128)(2,1)S(1)} %get-tuple-element.7.hot_ref, bf16[8,4,8,1920]{3,2,1,0:T(8,128)(2,1)S(1)} %bitcast.6), custom_call_target="tpu_custom_call" | custom-call | tf_op jit(solution)/shard_map/unpack/pallas_call | solution.py:230

commit v3 on v1

--- a/solution.py
+++ b/solution.py
@@ -65,13 +65,13 @@
     delta = total
     for rows in chunks:
         shifted = jnp.exp2(score_ref[rows] * scale - top)
-        score_ref[rows] = shifted
         total += eights(shifted, jnp.sum)
         delta += eights(shifted * dprob_ref[rows], jnp.sum)
-    weight = 1.0 / jnp.sum(total, axis=0, keepdims=True)
-    delta = jnp.sum(delta, axis=0, keepdims=True) * weight
+    total = jnp.sum(total, axis=0, keepdims=True)
+    delta = jnp.sum(delta, axis=0, keepdims=True) / total
+    top += jnp.log2(total)
     for rows in chunks:
-        probs = score_ref[rows] * weight
+        probs = jnp.exp2(score_ref[rows] * scale - top)
         probs_ref[rows, at] = probs.astype(jnp.bfloat16)
         dscores_ref[rows, at] = (probs * (dprob_ref[rows] - delta)).astype(jnp.bfloat16)
 

time: 75.6 us -> 75.8 us (level)
  no operation moved by 1% of the time
where the time goes in v3:
time: 75.8 us; the launch traced here: 75.6 us
  blocking collectives  67.1 us (89%)
  Pallas kernels  7.92 us (10%)
    all_to_all x1, blocking collectives, on_device(): lax.all_to_all(packed.reshape(peers, slice_rows, 4 * own), ('dp', 'seq'),...  39.7 us
    all_to_all x1, blocking collectives, on_device(): lax.all_to_all(grads.reshape(peers, slice_rows // folds, folds * 3 * own)...  27.4 us
    pallas_call x1, Pallas kernels, on_device(): pl.pallas_call(functools.partial(attention_kernel, heads, folds, slice_ro...  4.25 us
    pallas_call x1, Pallas kernels, on_device(): pl.pallas_call(functools.partial(pack_kernel, folds), out_shape=[bf16(dp_...  2.41 us

profile of v3, /device:TPU:1, one launch (start us, length us, event | category | flops | bytes accessed | tf_op | source)
XLA Modules:
  0.0 75.6 jit_solution(2145800601674489803)
XLA Ops:
  0.6 2.4 %pack.1 = (bf16[8,4,16,1280]{3,2,1,0:T(8,128)(2,1)S(1)}, bf16[512,128]{1,0:T(8,128)(2,1)S(1)}, bf16[512,128]{1,0:T(8,128)(2,1)S(1)}, bf16[128,128]{1,0:T(8,128)(2,1)S(1)}) custom-call(s32[1,512]{1,0:T(1,128)} %seg_ref.1, s32[1,128]{1,0:T(1,128)} %bitcast.9, bf16[128,1280]{1,0:T(8,128)(2,1)} %refs_0_.1, bf16[128,1280]{1,0:T(8,128)(2,1)} %refs_1_.1, ...), custom_call_target="tpu_custom_call" | custom-call | tf_op jit(solution)/shard_map/pack/pallas_call | solution.py:182
  3.1 39.7 %all_to_all.10 = bf16[32,16,1280]{2,1,0:T(8,128)(2,1)S(1)} all-to-all(bf16[32,16,1280]{2,1,0:T(8,128)(2,1)S(1)} %bitcast.8), channel_id=1, replica_groups=mesh['dp'=8,'seq'=4] {'dp','seq'}, dimensions={0} | all-to-all | bytes 2621440 | tf_op jit(solution)/shard_map/all_to_all | solution.py:201
  42.8 4.3 %attention.1 = bf16[256,1920]{1,0:T(8,128)(2,1)S(1)} custom-call(bf16[512,128]{1,0:T(8,128)(2,1)S(1)} %get-tuple-element.8.query_mark, bf16[512,128]{1,0:T(8,128)(2,1)S(1)} %get-tuple-element.9.key_mark, bf16[512,1280]{1,0:T(8,128)(2,1)S(1)} %bitcast.5), custom_call_target="tpu_custom_call" | custom-call | tf_op jit(solution)/shard_map/attention/pallas_call | solution.py:204
  47.0 27.4 %all_to_all.11 = bf16[32,8,1920]{2,1,0:T(8,128)(2,1)S(1)} all-to-all(bf16[32,8,1920]{2,1,0:T(8,128)(2,1)S(1)} %bitcast.7), channel_id=1, replica_groups=mesh['dp'=8,'seq'=4] {'dp','seq'}, dimensions={0} | all-to-all | bytes 1966080 | tf_op jit(solution)/shard_map/all_to_all | solution.py:218
  74.4 1.3 %unpack.1 = (bf16[128,1280]{1,0:T(8,128)(2,1)}, bf16[128,1280]{1,0:T(8,128)(2,1)}, bf16[128,1280]{1,0:T(8,128)(2,1)}) custom-call(bf16[128,128]{1,0:T(8,128)(2,1)S(1)} %get-tuple-element.7.hot_ref, bf16[8,4,8,1920]{3,2,1,0:T(8,128)(2,1)S(1)} %bitcast.6), custom_call_target="tpu_custom_call" | custom-call | tf_op jit(solution)/shard_map/unpack/pallas_call | solution.py:225

commit v4 on v1

v4 whole, which is shorter than its diff:
```python
import functools
import math

import jax
import jax.numpy as jnp
from jax import lax
from jax.experimental import pallas as pl
from jax.experimental.pallas import tpu as pltpu
from jax.sharding import PartitionSpec as P

HD = 80
NEG_FILL = -1e30
VMEM_LIMIT = 48 * 1024 * 1024
NT = (((1,), (1,)), ((), ()))
LANES = 128


def in_vmem(count):
    return [pl.BlockSpec(memory_space=pltpu.VMEM)] * count


def params():
    return pltpu.CompilerParams(vmem_limit_bytes=VMEM_LIMIT)


def bf16(*shape):
    return jax.ShapeDtypeStruct(shape, jnp.bfloat16)


def one_hot_columns(order_ref, rows):
    source = lax.broadcasted_iota(jnp.int32, (rows, rows), 0)
    return (source == order_ref[...]).astype(jnp.bfloat16)


def segment_marks(seg_ref):
    rows = seg_ref.shape[1]
    cut = jnp.sum(jnp.where(seg_ref[...] == 0, 1, 0))
    first = jnp.where(lax.broadcasted_iota(jnp.int32, (rows, 2), 0) < cut, 1.0, 0.0)
    own = jnp.where(lax.broadcasted_iota(jnp.int32, (rows, 2), 1) == 0, first, 1.0 - first)
    blank = jnp.zeros((rows, LANES - 2), jnp.float32)
    return tuple(
        jnp.concatenate([blank[:, :HD], mark, blank[:, HD:]], axis=1).astype(jnp.bfloat16)
        for mark in (own, (1.0 - own) * NEG_FILL)
    )


def segment_blocks(rows):
    quarter, low, high = rows // 4, rows * 3 // 8, rows * 5 // 8
    step = min(2 * quarter, 256)
    blocks = [(slice(at, at + step), slice(0, rows)) for at in range(quarter, 3 * quarter, step)]
    return blocks + [(slice(0, quarter), slice(0, high)), (slice(3 * quarter, rows), slice(low, rows))]


def eights(chunk, reduce):
    return reduce(chunk.reshape(chunk.shape[0] // 8, 8, chunk.shape[1]), axis=0)


def score_passes(score_ref, dprob_ref, at, keys, probs_ref, dscores_ref):
    scale = math.log2(math.e) / math.sqrt(HD)
    width = at.stop - at.start
    step = 64 * max(256 // width, 1)
    chunks = [slice(start, min(start + step, keys.stop)) for start in range(keys.start, keys.stop, step)]
    top = functools.reduce(jnp.maximum, [eights(score_ref[rows, at], jnp.max) for rows in chunks])
    top = jnp.max(top, axis=0, keepdims=True) * scale
    total = jnp.zeros((8, width), jnp.float32)
    delta = total
    for rows in chunks:
        shifted = jnp.exp2(score_ref[rows, at] * scale - top)
        score_ref[rows, at] = shifted
        total += eights(shifted, jnp.sum)
        delta += eights(shifted * dprob_ref[rows, at], jnp.sum)
    weight = 1.0 / jnp.sum(total, axis=0, keepdims=True)
    delta = jnp.sum(delta, axis=0, keepdims=True) * weight
    for rows in chunks:
        probs = score_ref[rows, at] * weight
        probs_ref[rows, at] = probs.astype(jnp.bfloat16)
        dscores_ref[rows, at] = (probs * (dprob_ref[rows, at] - delta)).astype(jnp.bfloat16)


def pack_kernel(folds, seg_ref, order_ref, *refs):
    inputs, (out_ref, query_mark, key_mark, hot_ref), (landed, seg_vmem, order_vmem, sems) = refs[:4], refs[4:8], refs[8:]
    rows, columns = inputs[0].shape
    seq_devs, slices = out_ref.shape[:2]
    slice_rows, own = rows // slices, columns // seq_devs
    copies = [
        pltpu.make_async_copy(order_ref, order_vmem, sems.at[4]),
        pltpu.make_async_copy(seg_ref, seg_vmem, sems.at[5]),
    ]
    copies += [pltpu.make_async_copy(ref, landed.at[index], sems.at[index]) for index, ref in enumerate(inputs)]
    for copy in copies:
        copy.start()
    copies[0].wait()
    columns_hot = one_hot_columns(order_vmem, rows)
    hot = columns_hot.T
    if folds > 1:
        places = columns_hot.astype(jnp.float32).T.reshape(rows // slice_rows, folds, slice_rows // folds, rows)
        places = [places[:, fold].reshape(rows // folds, rows) for fold in range(folds)]
        columns_hot = jnp.concatenate(places, axis=0).T.astype(jnp.bfloat16)
    hot_ref[...] = columns_hot
    copies[1].wait()
    query_mark[...], key_mark[...] = segment_marks(seg_vmem)
    for index in range(4):
        copies[2 + index].wait()
        permuted = jnp.dot(hot, landed[index], preferred_element_type=jnp.float32).astype(jnp.bfloat16)
        for peer in range(seq_devs):
            columns_of = permuted[:, peer * own : (peer + 1) * own]
            out_ref[peer, :, :, index * own : (index + 1) * own] = columns_of.reshape(slices, slice_rows, own)


def attention_kernel(
    heads, seq_devs, folds, slice_rows, query_mark, key_mark, x_ref, out_ref, scores, dprobs, probs, dscores
):
    rows = scores.shape[1]
    slices = rows // slice_rows // seq_devs
    width, part = 3 * heads * HD, slice_rows // folds
    inv_root = 1.0 / math.sqrt(HD)
    blocks = segment_blocks(rows)

    def piece(array, head):
        return x_ref[:, (array * heads + head) * HD : (array * heads + head + 1) * HD]

    def products(head):
        held[head] = tuple(piece(array, head) for array in range(4))
        query, key, value, grad = held[head]
        marked_query = jnp.concatenate([query, query_mark[:, HD:]], axis=1)
        marked_key = jnp.concatenate([key, key_mark[:, HD:]], axis=1)
        for at, keys in blocks:
            scores[head % 2, keys, at] = lax.dot_general(
                marked_key[keys], marked_query[at], NT, preferred_element_type=jnp.float32
            )
            dprobs[head % 2, keys, at] = lax.dot_general(
                value[keys], grad[at], NT, preferred_element_type=jnp.float32
            )

    def store(array, head, value):
        start = (array * heads + head) * HD
        for fold in range(folds):
            starts = [
                (device * slices + index) * slice_rows + fold * part
                for index in range(slices)
                for device in range(seq_devs)
            ]
            out_ref[:, fold * width + start : fold * width + start + HD] = jnp.concatenate(
                [value[row : row + part] for row in starts], axis=0
            ).astype(jnp.bfloat16)

    for slot in range(probs.shape[0]):
        for at, keys in blocks:
            for out in (slice(0, keys.start), slice(keys.stop, rows)):
                if out.stop > out.start:
                    zero = jnp.zeros((out.stop - out.start, at.stop - at.start), jnp.bfloat16)
                    probs[slot, out, at] = zero
                    dscores[slot, out, at] = zero
    held = {}
    products(0)
    for head in range(heads):
        if head + 1 < heads:
            products(head + 1)
        slot = head % probs.shape[0]
        for at, keys in blocks:
            score_passes(scores.at[head % 2], dprobs.at[head % 2], at, keys, probs.at[slot], dscores.at[slot])
        query, key, _, grad = held[head]
        grad_q = jnp.dot(key.T, dscores[slot], preferred_element_type=jnp.float32)
        store(0, head, grad_q.T * inv_root)
        store(1, head, jnp.dot(dscores[slot], query, preferred_element_type=jnp.float32) * inv_root)
        store(2, head, jnp.dot(probs[slot], grad, preferred_element_type=jnp.float32))


def unpack_kernel(folds, hot_ref, packed_ref, *outs):
    rows, columns = outs[0].shape
    seq_devs = packed_ref.shape[1]
    own = columns // seq_devs
    hot = hot_ref[...]
    for index, ref in enumerate(outs):
        whole = []
        for fold in range(folds):
            start = (fold * 3 + index) * own
            pieces = [
                packed_ref[:, peer, :, start : start + own].reshape(rows // folds, own) for peer in range(seq_devs)
            ]
            whole.append(jnp.concatenate(pieces, axis=1))
        ref[...] = jnp.dot(
            hot, jnp.concatenate(whole, axis=0), preferred_element_type=jnp.float32
        ).astype(jnp.bfloat16)


def on_device(queries, key_states, value_states, out_grads, row_order, segment_ids):
    rows, columns = queries.shape
    dp_devs, seq_devs = lax.axis_size("dp"), lax.axis_size("seq")
    own = columns // seq_devs
    heads = own // HD
    peers = dp_devs * seq_devs
    slice_rows = rows // dp_devs
    group_rows = rows * seq_devs
    folds = 2 if slice_rows % 16 == 0 and 3 * own % 128 else 1
    order = row_order.reshape(1, rows)
    arrays = (segment_ids, order, queries, key_states, value_states, out_grads)

    packed, query_mark, key_mark, hot = pl.pallas_call(
        functools.partial(pack_kernel, folds),
        out_shape=[
            bf16(seq_devs, dp_devs, slice_rows, 4 * own),
            bf16(group_rows, LANES),
            bf16(group_rows, LANES),
            bf16(rows, rows),
        ],
        in_specs=[pl.BlockSpec(memory_space=pltpu.HBM)] * 6,
        out_specs=in_vmem(4),
        scratch_shapes=[
            pltpu.VMEM((4, rows, columns), jnp.bfloat16),
            pltpu.VMEM((1, group_rows), jnp.int32),
            pltpu.VMEM((1, rows), jnp.int32),
            pltpu.SemaphoreType.DMA((6,)),
        ],
        compiler_params=params(),
        name="pack",
    )(*(pltpu.with_memory_space_constraint(array, pltpu.HBM) for array in arrays))
    moved = lax.all_to_all(
        packed.reshape(peers, slice_rows, 4 * own), ("seq", "dp"), split_axis=0, concat_axis=0, tiled=True
    )
    grads = pl.pallas_call(
        functools.partial(attention_kernel, heads, seq_devs, folds, slice_rows),
        out_shape=bf16(group_rows // folds, folds * 3 * own),
        in_specs=in_vmem(3),
        out_specs=in_vmem(1)[0],
        scratch_shapes=[
            pltpu.VMEM((min(heads, 2), group_rows, group_rows), jnp.float32),
            pltpu.VMEM((min(heads, 2), group_rows, group_rows), jnp.float32),
            pltpu.VMEM((min(heads, 2), group_rows, group_rows), jnp.bfloat16),
            pltpu.VMEM((min(heads, 2), group_rows, group_rows), jnp.bfloat16),
        ],
        compiler_params=params(),
        name="attention",
    )(query_mark, key_mark, moved.reshape(group_rows, 4 * own))
    returned = lax.all_to_all(
        grads.reshape(peers, slice_rows // folds, folds * 3 * own),
        ("dp", "seq"),
        split_axis=0,
        concat_axis=0,
        tiled=True,
    )
    return pl.pallas_call(
        functools.partial(unpack_kernel, folds),
        out_shape=[bf16(rows, columns)] * 3,
        in_specs=in_vmem(2),
        out_specs=in_vmem(3),
        compiler_params=params(),
        name="unpack",
    )(hot, returned.reshape(dp_devs, seq_devs, slice_rows // folds, folds * 3 * own))


def solution(mesh):
    rows = P(("dp", "seq"), None)
    return jax.shard_map(
        on_device,
        mesh=mesh,
        in_specs=(rows, rows, rows, rows, P(("dp", "seq")), P("dp", None)),
        out_specs=(rows, rows, rows),
        check_vma=False,
    )
```

time: 75.6 us -> 75.5 us (level)
    all_to_all x1, blocking collectives: 27.4 us -> 28.2 us  [on_device(): lax.all_to_all(grads.reshape(peers, slice_rows // folds, folds * 3 * own)...]
where the time goes in v4:
time: 75.5 us; the launch traced here: 75.3 us
  blocking collectives  67.2 us (89%)
  Pallas kernels  7.49 us (10%)
    all_to_all x1, blocking collectives, on_device(): lax.all_to_all(packed.reshape(peers, slice_rows, 4 * own), ('seq', 'dp'),...  39 us
    all_to_all x1, blocking collectives, on_device(): lax.all_to_all(grads.reshape(peers, slice_rows // folds, folds * 3 * own)...  28.2 us
    pallas_call x1, Pallas kernels, on_device(): pl.pallas_call(functools.partial(attention_kernel, heads, seq_devs, folds...  3.84 us
    pallas_call x1, Pallas kernels, on_device(): pl.pallas_call(functools.partial(pack_kernel, folds), out_shape=[bf16(seq...  2.4 us

profile of v4, /device:TPU:1, one launch (start us, length us, event | category | flops | bytes accessed | tf_op | source)
XLA Modules:
  0.0 75.3 jit_solution(13435085266659906344)
XLA Ops:
  0.6 2.4 %pack.1 = (bf16[4,8,16,1280]{3,2,1,0:T(8,128)(2,1)S(1)}, bf16[512,128]{1,0:T(8,128)(2,1)S(1)}, bf16[512,128]{1,0:T(8,128)(2,1)S(1)}, bf16[128,128]{1,0:T(8,128)(2,1)S(1)}) custom-call(s32[1,512]{1,0:T(1,128)} %seg_ref.1, s32[1,128]{1,0:T(1,128)} %bitcast.9, bf16[128,1280]{1,0:T(8,128)(2,1)} %refs_0_.1, bf16[128,1280]{1,0:T(8,128)(2,1)} %refs_1_.1, ...), custom_call_target="tpu_custom_call" | custom-call | tf_op jit(solution)/shard_map/pack/pallas_call | solution.py:199
  3.0 39.0 %all_to_all.10 = bf16[32,16,1280]{2,1,0:T(8,128)(2,1)S(1)} all-to-all(bf16[32,16,1280]{2,1,0:T(8,128)(2,1)S(1)} %bitcast.8), channel_id=1, replica_groups=mesh['dp'=8,'seq'=4] {'seq','dp'}, dimensions={0} | all-to-all | bytes 2621440 | tf_op jit(solution)/shard_map/all_to_all | solution.py:218
  42.0 3.8 %attention.1 = bf16[256,1920]{1,0:T(8,128)(2,1)S(1)} custom-call(bf16[512,128]{1,0:T(8,128)(2,1)S(1)} %get-tuple-element.8.query_mark, bf16[512,128]{1,0:T(8,128)(2,1)S(1)} %get-tuple-element.9.key_mark, bf16[512,1280]{1,0:T(8,128)(2,1)S(1)} %bitcast.5), custom_call_target="tpu_custom_call" | custom-call | tf_op jit(solution)/shard_map/attention/pallas_call | solution.py:221
  45.9 28.2 %all_to_all.11 = bf16[32,8,1920]{2,1,0:T(8,128)(2,1)S(1)} all-to-all(bf16[32,8,1920]{2,1,0:T(8,128)(2,1)S(1)} %bitcast.7), channel_id=1, replica_groups=mesh['dp'=8,'seq'=4] {'dp','seq'}, dimensions={0} | all-to-all | bytes 1966080 | tf_op jit(solution)/shard_map/all_to_all | solution.py:235
  74.1 1.3 %unpack.1 = (bf16[128,1280]{1,0:T(8,128)(2,1)}, bf16[128,1280]{1,0:T(8,128)(2,1)}, bf16[128,1280]{1,0:T(8,128)(2,1)}) custom-call(bf16[128,128]{1,0:T(8,128)(2,1)S(1)} %get-tuple-element.7.hot_ref, bf16[8,4,8,1920]{3,2,1,0:T(8,128)(2,1)S(1)} %bitcast.6), custom_call_target="tpu_custom_call" | custom-call | tf_op jit(solution)/shard_map/unpack/pallas_call | solution.py:242

commit v5 on v4

--- a/solution.py
+++ b/solution.py
@@ -58,7 +58,7 @@
 def score_passes(score_ref, dprob_ref, at, keys, probs_ref, dscores_ref):
     scale = math.log2(math.e) / math.sqrt(HD)
     width = at.stop - at.start
-    step = 64 * max(256 // width, 1)
+    step = 32 * max(256 // width, 1)
     chunks = [slice(start, min(start + step, keys.stop)) for start in range(keys.start, keys.stop, step)]
     top = functools.reduce(jnp.maximum, [eights(score_ref[rows, at], jnp.max) for rows in chunks])
     top = jnp.max(top, axis=0, keepdims=True) * scale
@@ -80,8 +80,8 @@
 def pack_kernel(folds, seg_ref, order_ref, *refs):
     inputs, (out_ref, query_mark, key_mark, hot_ref), (landed, seg_vmem, order_vmem, sems) = refs[:4], refs[4:8], refs[8:]
     rows, columns = inputs[0].shape
-    seq_devs, slices = out_ref.shape[:2]
-    slice_rows, own = rows // slices, columns // seq_devs
+    seq_devs, slice_rows = out_ref.shape[1:3]
+    own = columns // seq_devs
     copies = [
         pltpu.make_async_copy(order_ref, order_vmem, sems.at[4]),
         pltpu.make_async_copy(seg_ref, seg_vmem, sems.at[5]),
@@ -104,7 +104,7 @@
         permuted = jnp.dot(hot, landed[index], preferred_element_type=jnp.float32).astype(jnp.bfloat16)
         for peer in range(seq_devs):
             columns_of = permuted[:, peer * own : (peer + 1) * own]
-            out_ref[peer, :, :, index * own : (index + 1) * own] = columns_of.reshape(slices, slice_rows, own)
+            out_ref[:, peer, :, index * own : (index + 1) * own] = columns_of.reshape(-1, slice_rows, own)
 
 
 def attention_kernel(
@@ -117,7 +117,9 @@
     blocks = segment_blocks(rows)
 
     def piece(array, head):
-        return x_ref[:, (array * heads + head) * HD : (array * heads + head + 1) * HD]
+        at = slice((array * heads + head) * HD, (array * heads + head + 1) * HD)
+        starts = [(index * seq_devs + device) * slice_rows for device in range(seq_devs) for index in range(slices)]
+        return jnp.concatenate([x_ref[start : start + slice_rows, at] for start in starts], axis=0)
 
     def products(head):
         held[head] = tuple(piece(array, head) for array in range(4))
@@ -199,7 +201,7 @@
     packed, query_mark, key_mark, hot = pl.pallas_call(
         functools.partial(pack_kernel, folds),
         out_shape=[
-            bf16(seq_devs, dp_devs, slice_rows, 4 * own),
+            bf16(dp_devs, seq_devs, slice_rows, 4 * own),
             bf16(group_rows, LANES),
             bf16(group_rows, LANES),
             bf16(rows, rows),
@@ -216,7 +218,7 @@
         name="pack",
     )(*(pltpu.with_memory_space_constraint(array, pltpu.HBM) for array in arrays))
     moved = lax.all_to_all(
-        packed.reshape(peers, slice_rows, 4 * own), ("seq", "dp"), split_axis=0, concat_axis=0, tiled=True
+        packed.reshape(peers, slice_rows, 4 * own), ("dp", "seq"), split_axis=0, concat_axis=0, tiled=True
     )
     grads = pl.pallas_call(
         functools.partial(attention_kernel, heads, seq_devs, folds, slice_rows),

time: 75.5 us -> 75.4 us (level)
    all_to_all x1, blocking collectives: 28.2 us -> 27.4 us  [on_device(): lax.all_to_all(grads.reshape(peers, slice_rows // folds, folds * 3 * own)...]
where the time goes in v5:
time: 75.4 us; the launch traced here: 75.2 us
  blocking collectives  67.1 us (89%)
  Pallas kernels  7.44 us (10%)
    all_to_all x1, blocking collectives, on_device(): lax.all_to_all(packed.reshape(peers, slice_rows, 4 * own), ('dp', 'seq'),...  39.7 us
    all_to_all x1, blocking collectives, on_device(): lax.all_to_all(grads.reshape(peers, slice_rows // folds, folds * 3 * own)...  27.4 us
    pallas_call x1, Pallas kernels, on_device(): pl.pallas_call(functools.partial(attention_kernel, heads, seq_devs, folds...  3.78 us
    pallas_call x1, Pallas kernels, on_device(): pl.pallas_call(functools.partial(pack_kernel, folds), out_shape=[bf16(dp_...  2.4 us

profile of v5, /device:TPU:1, one launch (start us, length us, event | category | flops | bytes accessed | tf_op | source)
XLA Modules:
  0.0 75.2 jit_solution(2110933183610931089)
XLA Ops:
  0.6 2.4 %pack.1 = (bf16[8,4,16,1280]{3,2,1,0:T(8,128)(2,1)S(1)}, bf16[512,128]{1,0:T(8,128)(2,1)S(1)}, bf16[512,128]{1,0:T(8,128)(2,1)S(1)}, bf16[128,128]{1,0:T(8,128)(2,1)S(1)}) custom-call(s32[1,512]{1,0:T(1,128)} %seg_ref.1, s32[1,128]{1,0:T(1,128)} %bitcast.9, bf16[128,1280]{1,0:T(8,128)(2,1)} %refs_0_.1, bf16[128,1280]{1,0:T(8,128)(2,1)} %refs_1_.1, ...), custom_call_target="tpu_custom_call" | custom-call | tf_op jit(solution)/shard_map/pack/pallas_call | solution.py:201
  3.0 39.7 %all_to_all.10 = bf16[32,16,1280]{2,1,0:T(8,128)(2,1)S(1)} all-to-all(bf16[32,16,1280]{2,1,0:T(8,128)(2,1)S(1)} %bitcast.8), channel_id=1, replica_groups=mesh['dp'=8,'seq'=4] {'dp','seq'}, dimensions={0} | all-to-all | bytes 2621440 | tf_op jit(solution)/shard_map/all_to_all | solution.py:220
  42.8 3.8 %attention.1 = bf16[256,1920]{1,0:T(8,128)(2,1)S(1)} custom-call(bf16[512,128]{1,0:T(8,128)(2,1)S(1)} %get-tuple-element.8.query_mark, bf16[512,128]{1,0:T(8,128)(2,1)S(1)} %get-tuple-element.9.key_mark, bf16[512,1280]{1,0:T(8,128)(2,1)S(1)} %bitcast.5), custom_call_target="tpu_custom_call" | custom-call | tf_op jit(solution)/shard_map/attention/pallas_call | solution.py:223
  46.6 27.4 %all_to_all.11 = bf16[32,8,1920]{2,1,0:T(8,128)(2,1)S(1)} all-to-all(bf16[32,8,1920]{2,1,0:T(8,128)(2,1)S(1)} %bitcast.7), channel_id=1, replica_groups=mesh['dp'=8,'seq'=4] {'dp','seq'}, dimensions={0} | all-to-all | bytes 1966080 | tf_op jit(solution)/shard_map/all_to_all | solution.py:237
  73.9 1.3 %unpack.1 = (bf16[128,1280]{1,0:T(8,128)(2,1)}, bf16[128,1280]{1,0:T(8,128)(2,1)}, bf16[128,1280]{1,0:T(8,128)(2,1)}) custom-call(bf16[128,128]{1,0:T(8,128)(2,1)S(1)} %get-tuple-element.7.hot_ref, bf16[8,4,8,1920]{3,2,1,0:T(8,128)(2,1)S(1)} %bitcast.6), custom_call_target="tpu_custom_call" | custom-call | tf_op jit(solution)/shard_map/unpack/pallas_call | solution.py:244
